TPU v7x, 32 devices: a whole 2x2x4 slice. The times are simulated.
32 devices in a mesh: groups: 2 (over y), dom: 4 (over z), sub: 2 (over x), comp: 2 (over core).
Axes of the slice: x: 2, y: 2, z: 4, core: 2. Of those that a mesh axis runs over, the one named last changes fastest.
Arguments:
- displacement: float32 [3, 262144], P(None, ('groups', 'dom', 'sub', 'comp')), parts along dimension 1, may hold values from -6 to 6
- far_lists: int32 [128, 64], P(('groups', 'dom', 'sub', 'comp')), parts along dimension 0, may hold values from 0 to 8191, as said below
- far_counts: int32 [128], P(('groups', 'dom', 'sub', 'comp')), parts along dimension 0, may hold values from 0 to 64, as said below
- near_lists: int32 [128, 128], P(('groups', 'dom', 'sub', 'comp')), parts along dimension 0, may hold values from 0 to 8447, as said below
- near_counts: int32 [128], P(('groups', 'dom', 'sub', 'comp')), parts along dimension 0, may hold values from 1 to 128, as said below
- connectivity: int32 [125, 4096], P(None, ('groups', 'dom', 'sub', 'comp')), parts along dimension 1, may hold values from 0 to 8703, as said below
- inverse_jacobian: float32 [9, 4096], P(None, ('groups', 'dom', 'sub', 'comp')), parts along dimension 1, may hold values from -2 to 2
- lame_first: bfloat16 [125, 4096], P(None, ('groups', 'dom', 'sub', 'comp')), parts along dimension 1, may hold values from 0.0039978027 to 0.039794922
- lame_shear: bfloat16 [125, 4096], P(None, ('groups', 'dom', 'sub', 'comp')), parts along dimension 1, may hold values from 0.0039978027 to 0.039794922
Outputs:
- assembled: float32 [3, 262144], P(None, ('groups', 'dom', 'sub', 'comp')), parts along dimension 1
There are 2 independent parts, one for each index of `groups`. A program takes and returns all parts, laid end to end along the dimension named above; each array names one. Nothing has to cross between parts.
Inputs may be any that keep to these rules, and one draw needn't show every extreme that they name: far_counts of a device towards its own partition is 0 and towards every other partition 1 or more; some count reaches 64. Used entries of one far list are distinct owned nodes. `far_lists`: entries are owned node numbers of the sending device. `near_counts`: every near count is 1 or more, some reaches 128. `near_lists`: each used entry names an owned node or a used slot of the device's far_recv. `connectivity`: the first 64 elements of every device name only owned nodes (below 8192); the others name owned nodes or used ghost slots; an element may name a position more than once.
All inputs are finite; a program needn't handle non-finite values.
Results may differ from a plain program's by a relative error of at most 0.0003.
Values sent between devices are 32-bit elements; how exact they have to be, the bound alone decides.
A program may use at most 64 MiB of HBM per device.

v0:
```python
import math

import jax
import jax.numpy as jnp
import numpy as np
from jax import lax
from jax.sharding import PartitionSpec as P


def basis_tables():
    gll_points = np.array([-1.0, -math.sqrt(3.0 / 7.0), 0.0, math.sqrt(3.0 / 7.0), 1.0])
    inner_root = math.sqrt(5.0 - 2.0 * math.sqrt(10.0 / 7.0)) / 3.0
    outer_root = math.sqrt(5.0 + 2.0 * math.sqrt(10.0 / 7.0)) / 3.0
    gauss_points = np.array([-outer_root, -inner_root, 0.0, inner_root, outer_root])
    values = np.zeros((5, 5))
    slopes = np.zeros((5, 5))
    for q in range(5):
        for n in range(5):
            product = 1.0
            for m in range(5):
                if m != n:
                    product = (
                        product
                        * (gauss_points[q] - gll_points[m])
                        / (gll_points[n] - gll_points[m])
                    )
            values[q, n] = product
            total = 0.0
            for l in range(5):
                if l != n:
                    term = 1.0 / (gll_points[n] - gll_points[l])
                    for m in range(5):
                        if m != n and m != l:
                            term = (
                                term
                                * (gauss_points[q] - gll_points[m])
                                / (gll_points[n] - gll_points[m])
                            )
                    total = total + term
            slopes[q, n] = total
    return (values, slopes)


def factored_forward(nodal):
    values, slopes = basis_tables()
    values = jnp.asarray(values, jnp.float32)
    slopes = jnp.asarray(slopes, jnp.float32)
    elements = nodal.shape[-1]
    lattice = nodal.reshape(3, 5, 5, 5, elements)
    directions = []
    for r in range(3):
        factors = [slopes if d == r else values for d in range(3)]
        partial_sum = jnp.einsum(
            "an,cnjke->cajke", factors[0], lattice, precision=lax.Precision.HIGHEST
        )
        partial_sum = jnp.einsum(
            "bj,cajke->cabke", factors[1], partial_sum, precision=lax.Precision.HIGHEST
        )
        partial_sum = jnp.einsum(
            "dk,cabke->cabde", factors[2], partial_sum, precision=lax.Precision.HIGHEST
        )
        directions.append(partial_sum.reshape(3, 125, elements))
    return jnp.stack(directions, axis=1)


def factored_backward(tref):
    values, slopes = basis_tables()
    values = jnp.asarray(values, jnp.float32)
    slopes = jnp.asarray(slopes, jnp.float32)
    elements = tref.shape[-1]
    result = jnp.zeros((3, 5, 5, 5, elements), jnp.float32)
    for r in range(3):
        factors = [slopes if d == r else values for d in range(3)]
        lattice = tref[:, r].reshape(3, 5, 5, 5, elements)
        partial_sum = jnp.einsum(
            "an,cabde->cnbde", factors[0], lattice, precision=lax.Precision.HIGHEST
        )
        partial_sum = jnp.einsum(
            "bj,cnbde->cnjde", factors[1], partial_sum, precision=lax.Precision.HIGHEST
        )
        partial_sum = jnp.einsum(
            "dk,cnjde->cnjke", factors[2], partial_sum, precision=lax.Precision.HIGHEST
        )
        result = result + partial_sum
    return result.reshape(3, 125, elements)


def material(gref, jacobian, first_lame, shear_lame):
    gradient = jnp.sum(jacobian[None, :, :, None, :] * gref[:, :, None, :, :], axis=1)
    strain = 0.5 * (gradient + jnp.swapaxes(gradient, 0, 1))
    trace_sum = gradient[0, 0] + gradient[1, 1] + gradient[2, 2]
    identity = jnp.eye(3, dtype=jnp.float32)[:, :, None, None]
    stress = 2.0 * shear_lame * strain + first_lame * trace_sum * identity
    return jnp.sum(jacobian[None, :, :, None, :] * stress[:, None, :, :, :], axis=2)


def element_terms(source, links, jacobian9, first_raw, shear_raw, extent):
    elements = links.shape[1]
    nodal = source[:, links]
    jacobian = jacobian9.reshape(3, 3, elements)
    gref = factored_forward(nodal)
    tref = material(gref, jacobian, first_raw.astype(jnp.float32), shear_raw.astype(jnp.float32))
    element_out = factored_backward(tref)
    return jnp.zeros((3, extent), jnp.float32).at[:, links].add(element_out)


def near_send(buffer):
    return lax.all_to_all(buffer, ("sub", "comp"), split_axis=1, concat_axis=1, tiled=True)


def near_back(buffer):
    return lax.all_to_all(buffer, ("sub", "comp"), split_axis=1, concat_axis=1, tiled=True)


def local(
    displacement,
    far_lists,
    far_counts,
    near_lists,
    near_counts,
    connectivity,
    inverse_jacobian,
    lame_first,
    lame_shear,
):
    node_count = displacement.shape[1]
    n_dom = far_counts.shape[0]
    n_peers = near_counts.shape[0]
    cap_far = far_lists.shape[1]
    cap_near = near_lists.shape[1]
    far_mask = (jnp.arange(cap_far)[None, :] < far_counts[:, None]).astype(jnp.float32)
    near_mask = (jnp.arange(cap_near)[None, :] < near_counts[:, None]).astype(jnp.float32)
    far_buffer = displacement[:, far_lists] * far_mask[None]
    far_recv = lax.all_to_all(far_buffer, "dom", split_axis=1, concat_axis=1, tiled=True)
    stacked = jnp.concatenate([displacement, far_recv.reshape(3, n_dom * cap_far)], axis=1)
    near_buffer = stacked[:, near_lists] * near_mask[None]
    near_recv = near_send(near_buffer)
    local_values = jnp.concatenate([displacement, near_recv.reshape(3, n_peers * cap_near)], axis=1)
    local_extent = node_count + n_peers * cap_near
    local_sum = element_terms(
        local_values, connectivity, inverse_jacobian, lame_first, lame_shear, local_extent
    )
    ghost_sum = local_sum[:, node_count:].reshape(3, n_peers, cap_near)
    ghost_back = near_back(ghost_sum) * near_mask[None]
    stack_extent = node_count + n_dom * cap_far
    stack_sum = jnp.zeros((3, stack_extent), jnp.float32).at[:, near_lists].add(ghost_back)
    stack_sum = stack_sum.at[:, :node_count].add(local_sum[:, :node_count])
    far_part = stack_sum[:, node_count:].reshape(3, n_dom, cap_far)
    far_back = (
        lax.all_to_all(far_part, "dom", split_axis=1, concat_axis=1, tiled=True) * far_mask[None]
    )
    owner_sum = jnp.zeros((3, node_count), jnp.float32).at[:, far_lists].add(far_back)
    return stack_sum[:, :node_count] + owner_sum


def solution(mesh):
    in_specs = (
        P(None, ("groups", "dom", "sub", "comp")),
        P(("groups", "dom", "sub", "comp"), None),
        P(("groups", "dom", "sub", "comp")),
        P(("groups", "dom", "sub", "comp"), None),
        P(("groups", "dom", "sub", "comp")),
        P(None, ("groups", "dom", "sub", "comp")),
        P(None, ("groups", "dom", "sub", "comp")),
        P(None, ("groups", "dom", "sub", "comp")),
        P(None, ("groups", "dom", "sub", "comp")),
    )
    out_specs = P(None, ("groups", "dom", "sub", "comp"))
    return jax.shard_map(local, mesh=mesh, in_specs=in_specs, out_specs=out_specs, check_vma=False)
```

profile of v0, /device:TPU:0, one launch (start us, length us, event | category | flops | bytes accessed | tf_op | source)
XLA Modules:
  0.0 214.3 jit_solution(3810829920703738874)
XLA Ops:
  0.0 0.8 fusion.29
  0.8 0.7 compare_select_fusion.1
  1.6 3.4 %copy.116 = f32[3,8192]{0,1:T(8,128)} copy(f32[3,8192]{1,0:T(4,128)} %param.15) | data formatting | bytes 196608 | tf_op args[0]
  5.0 2.9 %gather_fusion = f32[256,3]{1,0:T(8,128)S(1)} fusion(f32[3,8192]{0,1:T(8,128)} %copy.116, s32[1024]{0:T(1024)S(1)} %pad_clamp_fusion.2), kind=kCustom, calls=%fused_computation | custom fusion | bytes 7168 | tf_op jit(solution)/shard_map/gather | solution.py:133
  8.0 0.7 reshape.178
  8.7 6.3 %all-to-all-start = ((f32[4,1,192]{2,1,0:T(1,128)}), f32[4,1,192]{2,1,0:T(1,128)S(1)}, u32[]{:S(2)}, u32[]{:S(2)}) async-start(f32[4,1,192]{2,1,0:T(1,128)} %reshape.178), calls=%async_computation | async-start | bytes 8192 | tf_op jit(solution)/shard_map/all_to_all | solution.py:134
  15.2 5.4 %all-to-all-done = f32[4,1,192]{2,1,0:T(1,128)S(1)} async-done(((f32[4,1,192]{2,1,0:T(1,128)}), f32[4,1,192]{2,1,0:T(1,128)S(1)}, u32[]{:S(2)}, u32[]{:S(2)}) %all-to-all-start) | async-done | bytes 3104 | tf_op jit(solution)/shard_map/all_to_all | solution.py:134
  20.6 0.5 broadcast.104
  21.1 0.6 reduce.8
  22.0 2.7 %copy.119 = f32[3,8448]{0,1:T(8,128)} copy(f32[3,8448]{1,0:T(4,128)S(1)} %pad_maximum_fusion.2) | data formatting | bytes 202752 | tf_op jit(solution)/shard_map/concatenate | solution.py:135
  24.7 3.3 %gather_fusion.1 = f32[512,3]{1,0:T(8,128)S(1)} fusion(f32[3,8448]{0,1:T(8,128)} %copy.119, s32[1024]{0:T(1024)S(1)} %pad_clamp_fusion.1), kind=kCustom, calls=%fused_computation.1 | custom fusion | bytes 14336 | tf_op jit(solution)/shard_map/gather | solution.py:136
  28.1 0.6 multiply_bitcast_fusion
  28.7 3.2 %all-to-all-start.1 = ((f32[3,4,128]{2,0,1:T(4,128)}), f32[3,4,128]{2,0,1:T(4,128)S(1)}, u32[]{:S(2)}, u32[]{:S(2)}) async-start(f32[3,4,128]{2,0,1:T(4,128)} %multiply_bitcast_fusion), calls=%async_computation.1 | async-start | bytes 16384 | tf_op jit(solution)/shard_map/all_to_all | solution.py:108
  32.0 3.7 %all-to-all-done.1 = f32[3,4,128]{2,0,1:T(4,128)S(1)} async-done(((f32[3,4,128]{2,0,1:T(4,128)}), f32[3,4,128]{2,0,1:T(4,128)S(1)}, u32[]{:S(2)}, u32[]{:S(2)}) %all-to-all-start.1) | async-done | bytes 6176 | tf_op jit(solution)/shard_map/all_to_all | solution.py:108
  35.8 2.8 %copy.121 = f32[3,8704]{0,1:T(8,128)} copy(f32[3,8704]{1,0:T(4,128)S(1)} %pad_maximum_fusion.1) | data formatting | bytes 208896 | tf_op jit(solution)/shard_map/concatenate | solution.py:138
  38.5 32.5 %gather_fusion.2 = f32[16000,3]{1,0:T(8,128)} fusion(f32[3,8704]{0,1:T(8,128)} %copy.121, s32[16384]{0:T(1024)S(1)} %pad_clamp_fusion), kind=kCustom, calls=%fused_computation.2 | custom fusion | bytes 448000 | tf_op jit(solution)/shard_map/gather | solution.py:99
  71.1 5.2 %copy.122 = f32[125,128,3]{1,0,2:T(8,128)S(1)} copy(f32[125,128,3]{2,1,0:T(8,128)} %bitcast.104) | data formatting | bytes 384000 | tf_op jit(solution)/shard_map/gather | solution.py:99
  76.3 0.4 convolution_bitcast_fusion.10
  76.7 0.4 convolution_bitcast_fusion.13
  77.1 0.4 convolution_bitcast_fusion.7
  77.5 0.4 convolution_bitcast_fusion.9
  78.0 0.4 convolution_bitcast_fusion.12
  78.4 0.4 convolution_bitcast_fusion.11
  78.8 0.4 convolution_bitcast_fusion.8
  80.3 0.5 convolution_bitcast_fusion.1
  80.7 0.5 convolution_bitcast_fusion
  81.2 0.5 convolution_bitcast_fusion.3
  81.7 0.5 convolution_bitcast_fusion.2
  82.2 0.4 convolution_bitcast_fusion.5
  82.7 0.5 convolution_bitcast_fusion.4
  83.1 0.5 fusion.13
  83.6 0.5 convolution_add_fusion.1
  84.0 0.5 fusion.4
  84.5 4.6 %copy.178 = f32[125,128,3]{2,1,0:T(8,128)} copy(f32[125,128,3]{1,0,2:T(8,128)S(1)} %bitcast.108) | data formatting | bytes 384000 | tf_op jit(solution)/shard_map/reshape | solution.py:85
  89.1 90.2 %scatter_custom_fusion = f32[3,8704]{0,1:T(8,128)} fusion(s32[16000]{0:T(1024)S(1)} %fusion.25, f32[16000,3]{1,0:T(8,128)} %bitcast.105, f32[]{:T(128)} %constant.47.clone.1), kind=kCustom, calls=%fused_computation.7 | custom fusion | flops 48000 | bytes 104960 | tf_op jit(solution)/shard_map/scatter-add | solution.py:104
  179.4 1.0 slice.72
  180.3 0.7 copy.152
  181.0 3.4 %all-to-all-start.2 = ((f32[3,4,128]{2,0,1:T(4,128)}), f32[3,4,128]{2,0,1:T(4,128)S(1)}, u32[]{:S(2)}, u32[]{:S(2)}) async-start(f32[3,4,128]{2,0,1:T(4,128)} %copy.152), calls=%async_computation.2 | async-start | bytes 16384 | tf_op jit(solution)/shard_map/all_to_all | solution.py:112
  184.5 0.7 compare_reduce_fusion
  185.2 2.9 %all-to-all-done.2 = f32[3,4,128]{2,0,1:T(4,128)S(1)} async-done(((f32[3,4,128]{2,0,1:T(4,128)}), f32[3,4,128]{2,0,1:T(4,128)S(1)}, u32[]{:S(2)}, u32[]{:S(2)}) %all-to-all-start.2) | async-done | bytes 6176 | tf_op jit(solution)/shard_map/all_to_all | solution.py:112
  188.2 4.5 %scatter_custom_fusion.1 = f32[3,8448]{0,1:T(8,128)} fusion(s32[512]{0:T(512)S(1)} %fusion.28, f32[512,3]{1,0:T(8,128)S(1)} %copy.153, f32[]{:T(128)} %constant.47.clone.1), kind=kCustom, calls=%fused_computation.9 | custom fusion | flops 1536 | bytes 101380 | tf_op jit(solution)/shard_map/scatter-add | solution.py:146
  192.7 0.9 slice.75
  193.7 0.7 reshape.180
  194.4 3.2 %all-to-all-start.3 = ((f32[4,1,192]{2,1,0:T(1,128)}), f32[4,1,192]{2,1,0:T(1,128)S(1)}, u32[]{:S(2)}, u32[]{:S(2)}) async-start(f32[4,1,192]{2,1,0:T(1,128)} %reshape.180), calls=%async_computation.3 | async-start | bytes 8192 | tf_op jit(solution)/shard_map/all_to_all | solution.py:150
  197.7 6.4 %add_select_fusion = f32[3,8192]{0,1:T(8,128)} fusion(f32[3,8704]{0,1:T(8,128)} %scatter_custom_fusion, f32[3,8448]{0,1:T(8,128)} %scatter_custom_fusion.1, pred[]{:T(512)} %compare_reduce_fusion), kind=kLoop, calls=%fused_computation.6 | loop fusion | flops 49152 | bytes 294913 | tf_op jit(solution)/shard_map/slice | solution.py:153
  204.1 0.6 reduce.9
  204.9 5.9 %scatter_fusion = f32[3,8192]{0,1:T(8,128)} fusion(f32[3,8192]{0,1:T(8,128)} %add_select_fusion, s32[256]{0:T(256)S(1)} %reshape.105, f32[256,3]{1,0:T(8,128)S(1)} %bitcast.112), kind=kCustom, calls=%fused_computation.5 | custom fusion | flops 768 | bytes 10240 | tf_op jit(solution)/shard_map/scatter-add | solution.py:152
  210.8 3.5 %copy.157 = f32[3,8192]{1,0:T(4,128)} copy(f32[3,8192]{0,1:T(8,128)} %scatter_fusion) | data formatting | bytes 196608 | tf_op jit(solution)/shard_map/scatter-add | solution.py:152
  (57 shorter events, 2.3 us)
Async XLA Ops:
  0.0 22.0 %copy-start = (f32[3,8192]{1,0:T(4,128)S(1)}, f32[3,8192]{1,0:T(4,128)}, u32[]{:S(2)}) copy-start(f32[3,8192]{1,0:T(4,128)} %param.15) | copy-start | bytes 294916
  0.0 15.1 %copy-start.7 = (s32[4,128]{1,0:T(4,128)S(1)}, s32[4,128]{1,0:T(4,128)}, u32[]{:S(2)}) copy-start(s32[4,128]{1,0:T(4,128)} %param.18) | copy-start | bytes 6148
  0.0 15.1 %copy-start.8 = (s32[4]{0:T(128)S(1)}, s32[4]{0:T(128)}, u32[]{:S(2)}) copy-start(s32[4]{0:T(128)} %param.19) | copy-start | bytes 52
  0.0 15.1 %copy-start.3 = (s32[125,128]{1,0:T(8,128)S(1)}, s32[125,128]{1,0:T(8,128)}, u32[]{:S(2)}) copy-start(s32[125,128]{1,0:T(8,128)} %param.20) | copy-start | bytes 192004
  1.6 30.4 %copy-start.6 = (f32[9,128]{1,0:T(8,128)S(1)}, f32[9,128]{1,0:T(8,128)}, u32[]{:S(2)}) copy-start(f32[9,128]{1,0:T(8,128)} %param.21) | copy-start | bytes 13828
  1.6 30.4 %copy-start.4 = (bf16[125,128]{1,0:T(8,128)(2,1)S(1)}, bf16[125,128]{1,0:T(8,128)(2,1)}, u32[]{:S(2)}) copy-start(bf16[125,128]{1,0:T(8,128)(2,1)} %param.23) | copy-start | bytes 96004
  8.7 11.9 %all-to-all-start = ((f32[4,1,192]{2,1,0:T(1,128)}), f32[4,1,192]{2,1,0:T(1,128)S(1)}, u32[]{:S(2)}, u32[]{:S(2)}) async-start(f32[4,1,192]{2,1,0:T(1,128)} %reshape.178), calls=%async_computation | async-start | bytes 8192 | tf_op jit(solution)/shard_map/all_to_all | solution.py:134
  28.7 7.0 %all-to-all-start.1 = ((f32[3,4,128]{2,0,1:T(4,128)}), f32[3,4,128]{2,0,1:T(4,128)S(1)}, u32[]{:S(2)}, u32[]{:S(2)}) async-start(f32[3,4,128]{2,0,1:T(4,128)} %multiply_bitcast_fusion), calls=%async_computation.1 | async-start | bytes 16384 | tf_op jit(solution)/shard_map/all_to_all | solution.py:108
  71.1 5.2 %copy-start.1 = (f32[5,5,1,1,1]{1,0,4,3,2:T(8,128)S(1)}, f32[5,5,1,1,1]{1,0,4,3,2:T(8,128)}, u32[]{:S(2)}) copy-start(f32[5,5,1,1,1]{1,0,4,3,2:T(8,128)} %constant.58) | copy-start | bytes 304
  71.1 5.7 %copy-start.2 = (f32[5,5,1,1,1]{1,0,4,3,2:T(8,128)S(1)}, f32[5,5,1,1,1]{1,0,4,3,2:T(8,128)}, u32[]{:S(2)}) copy-start(f32[5,5,1,1,1]{1,0,4,3,2:T(8,128)} %constant.57) | copy-start | bytes 304
  76.2 3.6 %copy-start.5 = (bf16[125,128]{1,0:T(8,128)(2,1)S(1)}, bf16[125,128]{1,0:T(8,128)(2,1)}, u32[]{:S(2)}) copy-start(bf16[125,128]{1,0:T(8,128)(2,1)} %param.22) | copy-start | bytes 96004
  181.0 7.0 %all-to-all-start.2 = ((f32[3,4,128]{2,0,1:T(4,128)}), f32[3,4,128]{2,0,1:T(4,128)S(1)}, u32[]{:S(2)}, u32[]{:S(2)}) async-start(f32[3,4,128]{2,0,1:T(4,128)} %copy.152), calls=%async_computation.2 | async-start | bytes 16384 | tf_op jit(solution)/shard_map/all_to_all | solution.py:112
  194.4 9.7 %all-to-all-start.3 = ((f32[4,1,192]{2,1,0:T(1,128)}), f32[4,1,192]{2,1,0:T(1,128)S(1)}, u32[]{:S(2)}, u32[]{:S(2)}) async-start(f32[4,1,192]{2,1,0:T(1,128)} %reshape.180), calls=%async_computation.3 | async-start | bytes 8192 | tf_op jit(solution)/shard_map/all_to_all | solution.py:150
where the time goes:
time: 215 us; the launch traced here: 214 us
  other arithmetic  112 us (52%)
  local copies, waits for them, and re-layouts  66.5 us (31%)
  starting transfers between devices  16.3 us (8%)
  waiting for transfers between devices  12.1 us (6%)
  matrix products  7.35 us (3%)
    scatter-add x1, other arithmetic, element_terms(): return jnp.zeros((3, extent), jnp.float32).at[:, links].add(element_out)  90.2 us
    gather x2, local copies, waits for them, and re-layouts, element_terms(): nodal = source[:, links]  37.7 us
    slice x1, other arithmetic, local(): return stack_sum[:, :node_count] + owner_sum  6.43 us
    all_to_all x1, starting transfers between devices, local(): lax.all_to_all(far_buffer, 'dom', split_axis=1, concat_axis=1, tiled=True)  6.35 us
    scatter-add x1, other arithmetic, local(): jnp.zeros((3, node_count), jnp.float32).at[:, far_lists].add(far_back)  5.89 us
    all_to_all x1, waiting for transfers between devices, local(): lax.all_to_all(far_buffer, 'dom', split_axis=1, concat_axis=1, tiled=True)  5.43 us
    unnamed x23, local copies, waits for them, and re-layouts  5.03 us
    reshape x2, local copies, waits for them, and re-layouts, factored_backward(): return result.reshape(3, 125, elements)  4.59 us
  transfers between devices with their start and end apart: 4, of which 3 were waited for; matrix products, arithmetic and copies ran while one was open for 3% of the time, Pallas kernels for 0%

commit v1 on v0

v1 whole, which is shorter than its diff:
```python
import functools
import math

import jax
import jax.numpy as jnp
import numpy as np
from jax import lax
from jax.experimental import pallas as pl
from jax.experimental.pallas import tpu as pltpu
from jax.sharding import PartitionSpec as P

F32 = jnp.float32
BF16 = jnp.bfloat16
LANES = 128
ROWS = 64
NOWHERE = 16383
HIGH = 48
MESH = pl.DeviceIdType.MESH


def basis_tables():
    gll_points = np.array([-1.0, -math.sqrt(3.0 / 7.0), 0.0, math.sqrt(3.0 / 7.0), 1.0])
    inner_root = math.sqrt(5.0 - 2.0 * math.sqrt(10.0 / 7.0)) / 3.0
    outer_root = math.sqrt(5.0 + 2.0 * math.sqrt(10.0 / 7.0)) / 3.0
    gauss_points = np.array([-outer_root, -inner_root, 0.0, inner_root, outer_root])
    values = np.zeros((5, 5))
    slopes = np.zeros((5, 5))
    for q in range(5):
        for n in range(5):
            product = 1.0
            for m in range(5):
                if m != n:
                    product = (
                        product
                        * (gauss_points[q] - gll_points[m])
                        / (gll_points[n] - gll_points[m])
                    )
            values[q, n] = product
            total = 0.0
            for l in range(5):
                if l != n:
                    term = 1.0 / (gll_points[n] - gll_points[l])
                    for m in range(5):
                        if m != n and m != l:
                            term = (
                                term
                                * (gauss_points[q] - gll_points[m])
                                / (gll_points[n] - gll_points[m])
                            )
                    total = total + term
            slopes[q, n] = total
    return (values, slopes)


def split_tables():
    values, slopes = basis_tables()
    forward = np.zeros((3, LANES, LANES), np.float32)
    for r in range(3):
        factors = [slopes if d == r else values for d in range(3)]
        forward[r, :125, :125] = np.kron(np.kron(factors[0], factors[1]), factors[2])
    stacked = forward.reshape(3 * LANES, LANES)
    top = stacked.astype(jnp.bfloat16)
    rest = (stacked - top.astype(np.float32)).astype(jnp.bfloat16)
    fwd = np.concatenate([top, rest, top], axis=1)
    bwd = np.concatenate([top.T, rest.T, top.T], axis=1)
    return np.ascontiguousarray(fwd), np.ascontiguousarray(bwd)


def split(x):
    top = x.astype(BF16)
    return top, (x - top.astype(F32)).astype(BF16)


def onehot(rows, key):
    grid = lax.broadcasted_iota(jnp.int32, (rows, key.shape[1]), 0)
    return jnp.where(grid == key, 1.0, 0.0).astype(BF16)


def pick(table, rows):
    found = [[], [], []]
    for at in range(0, len(rows), 2):
        pair = jnp.concatenate(rows[at : at + 2], axis=1)
        high = onehot(LANES, pair >> 7)
        dense = jnp.dot(
            table, jnp.concatenate([high, high], axis=0), preferred_element_type=F32
        )
        low = lax.broadcasted_iota(jnp.int32, (LANES, 2 * LANES), 0) == (pair & 127)
        for c in range(3):
            part = dense[c * LANES : (c + 1) * LANES]
            line = jnp.sum(jnp.where(low, part, 0.0), axis=0, keepdims=True)
            found[c] += [line[:, :LANES], line[:, LANES:]]
    return found


def spread(rows, values):
    key = jnp.concatenate(rows, axis=1)
    low = onehot(2 * LANES, key & 255)
    high = onehot(HIGH, key >> 8)
    parts = []
    for c in range(3):
        top, rest = split(jnp.concatenate(values[c], axis=1))
        parts += [high * top, high * rest]
    return lax.dot_general(
        jnp.concatenate(parts, axis=0),
        low,
        (((1,), (1,)), ((), ())),
        preferred_element_type=F32,
    )


def joined(acc, c):
    return acc[2 * HIGH * c : 2 * HIGH * c + HIGH] + acc[2 * HIGH * c + HIGH : 2 * HIGH * (c + 1)]


def kernel(
    n_dom,
    n_sub,
    n_comp,
    far_counts,
    near_counts,
    disp,
    far_lists,
    near_lists,
    conn,
    jac,
    lame_first,
    lame_shear,
    fwd,
    bwd,
    out,
    tab,
    table,
    far_index,
    index,
    nodal,
    first,
    shear,
    acc_in,
    acc_out,
    far_out,
    far_in,
    near_out,
    near_in,
    ghost_out,
    ghost_in,
    back_out,
    back_in,
    send_far,
    recv_far,
    send_near,
    recv_near,
    send_ghost,
    recv_ghost,
    send_back,
    recv_back,
):
    n_peers = n_sub * n_comp
    owned = disp.shape[1] // LANES
    dom = lax.axis_index("dom")
    peer = lax.axis_index("sub") * n_comp + lax.axis_index("comp")

    def dom_id(step):
        return {"dom": lax.rem(dom + step, n_dom)}

    def peer_id(step):
        other = lax.rem(peer + step, n_peers)
        return {"sub": other // n_comp, "comp": lax.rem(other, n_comp)}

    def far_copies(source, target, send, recv):
        return [
            pltpu.make_async_remote_copy(
                src_ref=source.at[lax.rem(dom + step, n_dom)],
                dst_ref=target.at[dom],
                send_sem=send.at[step],
                recv_sem=recv.at[step],
                device_id=dom_id(step),
                device_id_type=MESH,
            )
            for step in range(1, n_dom)
        ]

    def near_copies(source, target, send, recv):
        return [
            pltpu.make_async_remote_copy(
                src_ref=source.at[lax.rem(peer + step, n_peers)],
                dst_ref=target.at[peer],
                send_sem=send.at[step],
                recv_sem=recv.at[step],
                device_id=peer_id(step),
                device_id_type=MESH,
            )
            for step in range(1, n_peers)
        ]

    barrier = pltpu.get_barrier_semaphore()
    for step in range(1, n_dom):
        pl.semaphore_signal(barrier, inc=1, device_id=dom_id(step), device_id_type=MESH)
    for step in range(1, n_peers):
        pl.semaphore_signal(barrier, inc=1, device_id=peer_id(step), device_id_type=MESH)

    lane8 = lax.broadcasted_iota(jnp.int32, (8, LANES), 1)
    lane = lax.broadcasted_iota(jnp.int32, (1, LANES), 1)

    for c in range(3):
        tab[c, owned:, :] = jnp.zeros((LANES - owned, LANES), F32)
        for h in range(owned):
            tab[c, h : h + 1, :] = disp[c : c + 1, h * LANES : (h + 1) * LANES]

    def turn():
        for c in range(3):
            top, rest = split(tab[c].T)
            table[c * LANES : (c + 1) * LANES, :LANES] = top
            table[c * LANES : (c + 1) * LANES, LANES:] = rest

    turn()

    far_index[...] = jnp.zeros_like(far_index)
    far_index[:n_dom, :64] = far_lists[...]
    listed = far_index[...]
    lane_f = lax.broadcasted_iota(jnp.int32, listed.shape, 1)
    listed = jnp.where(lane_f < 64, listed, pltpu.roll(listed, 64, 1))
    far_rows = [
        jnp.where((lane & 63) < far_counts[p], listed[p : p + 1], NOWHERE) for p in range(n_dom)
    ]
    near_rows = [
        jnp.where(lane < near_counts[t], near_lists[t : t + 1, :], NOWHERE)
        for t in range(n_peers)
    ]

    far_out[...] = jnp.zeros_like(far_out)
    near_out[...] = jnp.zeros_like(near_out)
    ghost_out[...] = jnp.zeros_like(ghost_out)
    back_out[...] = jnp.zeros_like(back_out)

    found = pick(table[...], far_rows)
    for p in range(n_dom):
        for c in range(3):
            far_out[p, c : c + 1, :] = found[c][p]
    far_in[dom] = jnp.zeros((8, LANES), F32)
    back_in[dom] = jnp.zeros((8, LANES), F32)

    pl.semaphore_wait(barrier, n_dom - 1 + n_peers - 1)
    sends = far_copies(far_out, far_in, send_far, recv_far)
    for copy in sends:
        copy.start()

    tab_rows = jnp.full((8, LANES), NOWHERE, jnp.int32)
    index[0, 120:128, :] = tab_rows
    index[0, :125, :] = conn[...]
    low_half = index[0, :ROWS, :]
    high_half = index[0, ROWS:, :]
    lane64 = lax.broadcasted_iota(jnp.int32, (ROWS, LANES), 1)
    packed_in = jnp.where(lane64 < 64, low_half, pltpu.roll(high_half, 64, 1))
    packed_out = jnp.where(lane64 < 64, pltpu.roll(low_half, 64, 1), high_half)
    index[1, :ROWS, :] = packed_in
    index[1, ROWS:, :] = packed_out

    first[120:128, :] = jnp.zeros((8, LANES), F32)
    shear[120:128, :] = jnp.zeros((8, LANES), F32)
    first[:125, :] = lame_first[...].astype(F32)
    shear[:125, :] = lame_shear[...].astype(F32)

    def gather(half):
        def body(step, _):
            at = pl.multiple_of(half * ROWS + step * 8, 8)
            block = index[1, pl.ds(at, 8), :]
            got = pick(table[...], [block[r : r + 1] for r in range(8)])
            for c in range(3):
                nodal[c, pl.ds(at, 8), :] = jnp.concatenate(got[c], axis=0)
            return 0

        lax.fori_loop(0, ROWS // 8, body, 0)

    def scatter(half, acc):
        acc[...] = jnp.zeros_like(acc)

        def body(step, _):
            at = pl.multiple_of(half * ROWS + step * 8, 8)
            block = index[1, pl.ds(at, 8), :]
            terms = [nodal[c, pl.ds(at, 8), :] for c in range(3)]
            acc[...] += spread(
                [block[r : r + 1] for r in range(8)],
                [[terms[c][r : r + 1] for r in range(8)] for c in range(3)],
            )
            return 0

        lax.fori_loop(0, ROWS // 8, body, 0)

    def elements(half):
        rows = slice(half * ROWS, (half + 1) * ROWS)
        columns = []
        for c in range(3):
            packed = nodal[c, rows, :]
            turned = pltpu.roll(packed, 64, 1)
            columns.append(jnp.concatenate([packed, turned], axis=0))
        top, rest = split(jnp.concatenate(columns, axis=1))
        gref = jnp.dot(
            fwd[...], jnp.concatenate([top, top, rest], axis=0), preferred_element_type=F32
        )
        jacobian = jac[...]
        lam = first[...]
        mu = shear[...]
        if half == 1:
            jacobian = pltpu.roll(jacobian, 64, 1)
            lam = pltpu.roll(lam, 64, 1)
            mu = pltpu.roll(mu, 64, 1)
        factor = [[jacobian[3 * r + i : 3 * r + i + 1] for i in range(3)] for r in range(3)]
        ref = [
            [
                gref[r * LANES : (r + 1) * LANES, c * LANES : (c + 1) * LANES]
                for r in range(3)
            ]
            for c in range(3)
        ]
        grad = [
            [
                factor[0][i] * ref[c][0] + factor[1][i] * ref[c][1] + factor[2][i] * ref[c][2]
                for i in range(3)
            ]
            for c in range(3)
        ]
        trace = lam * (grad[0][0] + grad[1][1] + grad[2][2])
        stress = [[None] * 3 for _ in range(3)]
        for c in range(3):
            stress[c][c] = 2.0 * mu * grad[c][c] + trace
            for i in range(c + 1, 3):
                stress[c][i] = stress[i][c] = mu * (grad[c][i] + grad[i][c])
        tref = jnp.concatenate(
            [
                jnp.concatenate(
                    [
                        factor[r][0] * stress[c][0]
                        + factor[r][1] * stress[c][1]
                        + factor[r][2] * stress[c][2]
                        for c in range(3)
                    ],
                    axis=1,
                )
                for r in range(3)
            ],
            axis=0,
        )
        top, rest = split(tref)
        result = jnp.dot(
            bwd[...], jnp.concatenate([top, top, rest], axis=0), preferred_element_type=F32
        )
        for c in range(3):
            part = result[:, c * LANES : (c + 1) * LANES]
            nodal[c, rows, :] = jnp.where(
                lane64 < 64, part[:ROWS], pltpu.roll(part[ROWS:], 64, 1)
            )

    gather(0)

    for copy in sends:
        copy.wait()
    for j in range(n_dom // 2):
        for c in range(3):
            tab[c, owned + j : owned + j + 1, :] = jnp.where(
                lane < 64, far_in[2 * j, c : c + 1, :], far_in[2 * j + 1, c : c + 1, :]
            )
    turn()
    found = pick(table[...], near_rows)
    for t in range(n_peers):
        for c in range(3):
            near_out[t, c : c + 1, :] = found[c][t]
    near_in[peer] = near_out[peer]
    sends = near_copies(near_out, near_in, send_near, recv_near)
    for copy in sends:
        copy.start()

    elements(0)

    for copy in sends:
        copy.wait()
    for c in range(3):
        tab[c, owned:, :] = jnp.zeros((LANES - owned, LANES), F32)
        for s in range(n_peers):
            tab[c, owned + s : owned + s + 1, :] = near_in[s, c : c + 1, :]
    turn()
    gather(1)
    elements(1)
    scatter(1, acc_out)
    outer = acc_out[...]
    kept = owned // 2
    for c in range(3):
        whole = joined(outer, c)
        for s in range(n_peers):
            half = (s % 2) * LANES
            ghost_out[s, c : c + 1, :] = whole[kept + s // 2 : kept + s // 2 + 1, half : half + LANES]
    ghost_in[peer] = ghost_out[peer]
    sends = near_copies(ghost_out, ghost_in, send_ghost, recv_ghost)
    for copy in sends:
        copy.start()

    scatter(0, acc_in)

    for copy in sends:
        copy.wait()
    ghost = spread(
        near_rows, [[ghost_in[t, c : c + 1, :] for t in range(n_peers)] for c in range(3)]
    )
    for c in range(3):
        whole = joined(ghost, c)
        for p in range(n_dom):
            half = ((p // 2) % 2) * LANES
            back_out[p, c : c + 1, :] = whole[kept + p // 4 : kept + p // 4 + 1, half : half + LANES]
    sends = far_copies(back_out, back_in, send_back, recv_back)
    for copy in sends:
        copy.start()
    total = acc_in[...] + acc_out[...] + ghost
    mine = (lane >> 6) == lax.rem(dom, 2)
    back_rows = [jnp.where(mine, far_rows[p], NOWHERE) for p in range(n_dom)]
    for copy in sends:
        copy.wait()
    total = total + spread(
        back_rows, [[back_in[p, c : c + 1, :] for p in range(n_dom)] for c in range(3)]
    )
    for c in range(3):
        whole = joined(total, c)
        for q in range(kept):
            out[c : c + 1, q * 2 * LANES : (q + 1) * 2 * LANES] = whole[q : q + 1]


def local(
    n_dom,
    n_sub,
    n_comp,
    displacement,
    far_lists,
    far_counts,
    near_lists,
    near_counts,
    connectivity,
    inverse_jacobian,
    lame_first,
    lame_shear,
):
    n_peers = n_sub * n_comp
    fwd, bwd = split_tables()
    smem = pl.BlockSpec(memory_space=pltpu.SMEM)
    vmem = pl.BlockSpec(memory_space=pltpu.VMEM)
    far_slots = pltpu.VMEM((n_dom, 8, LANES), F32)
    near_slots = pltpu.VMEM((n_peers, 8, LANES), F32)
    return pl.pallas_call(
        functools.partial(kernel, n_dom, n_sub, n_comp),
        out_shape=jax.ShapeDtypeStruct(displacement.shape, F32),
        in_specs=[smem] * 2 + [vmem] * 9,
        out_specs=vmem,
        scratch_shapes=[
            pltpu.VMEM((3, LANES, LANES), F32),
            pltpu.VMEM((3 * LANES, 2 * LANES), BF16),
            pltpu.VMEM((max(8, n_dom), LANES), jnp.int32),
            pltpu.VMEM((2, 2 * ROWS, LANES), jnp.int32),
            pltpu.VMEM((3, 2 * ROWS, LANES), F32),
            pltpu.VMEM((LANES, LANES), F32),
            pltpu.VMEM((LANES, LANES), F32),
            pltpu.VMEM((6 * HIGH, 2 * LANES), F32),
            pltpu.VMEM((6 * HIGH, 2 * LANES), F32),
            far_slots,
            far_slots,
            near_slots,
            near_slots,
            near_slots,
            near_slots,
            far_slots,
            far_slots,
        ]
        + [pltpu.SemaphoreType.DMA((n_dom,))] * 2
        + [pltpu.SemaphoreType.DMA((n_peers,))] * 4
        + [pltpu.SemaphoreType.DMA((n_dom,))] * 2,
        compiler_params=pltpu.CompilerParams(
            collective_id=0, has_side_effects=True, vmem_limit_bytes=32 * 1024 * 1024
        ),
    )(
        far_counts,
        near_counts,
        displacement,
        far_lists,
        near_lists,
        connectivity,
        inverse_jacobian,
        lame_first,
        lame_shear,
        jnp.asarray(fwd),
        jnp.asarray(bwd),
    )


def solution(mesh):
    spread_axes = ("groups", "dom", "sub", "comp")
    rows = P(spread_axes, None)
    columns = P(None, spread_axes)
    flat = P(spread_axes)
    in_specs = (columns, rows, flat, rows, flat, columns, columns, columns, columns)
    sizes = (mesh.shape["dom"], mesh.shape["sub"], mesh.shape["comp"])
    return jax.shard_map(
        functools.partial(local, *sizes),
        mesh=mesh,
        in_specs=in_specs,
        out_specs=columns,
        check_vma=False,
    )
```

time: 215 us -> 37.2 us (0.17)
  other arithmetic: 112 us -> 0 us
  local copies, waits for them, and re-layouts: 66.5 us -> 9.21 us
  Pallas kernels: 0 us -> 27.4 us
  starting transfers between devices: 16.3 us -> 0 us
  waiting for transfers between devices: 12.1 us -> 0 us
  matrix products: 7.35 us -> 0 us
    scatter-add x3 -> x0, other arithmetic: 101 us -> none  [the longest x1 90.2 us: element_terms(): return jnp.zeros((3, extent), jnp.float32).at[:, links].add(element_out)]
    gather x6 -> x0, local copies, waits for them, and re-layouts: 44.1 us -> none  [the longest x2 37.7 us: element_terms(): nodal = source[:, links]]
    pallas_call x0 -> x1, Pallas kernels: none -> 27.4 us  [local(): pl.pallas_call(functools.partial(kernel, n_dom, n_sub, n_comp), out_shape...]
    all_to_all x4 -> x0, starting transfers between devices: 16.3 us -> none  [the longest x1 6.35 us: local(): lax.all_to_all(far_buffer, 'dom', split_axis=1, concat_axis=1, tiled=True)]
    all_to_all x4 -> x0, waiting for transfers between devices: 12.1 us -> none  [the longest x1 5.43 us: local(): lax.all_to_all(far_buffer, 'dom', split_axis=1, concat_axis=1, tiled=True)]
    dot_general x17 -> x0, matrix products: 7.35 us -> none  [the longest x3 1.37 us: factored_backward(): jnp.einsum('dk,cnjde->cnjke', factors[2], partial_sum, precision=lax.Prec...]
    slice x1 -> x0, other arithmetic: 6.43 us -> none  [local(): return stack_sum[:, :node_count] + owner_sum]
    reshape x6 -> x0, local copies, waits for them, and re-layouts: 5.51 us -> none  [the longest x2 4.59 us: factored_backward(): return result.reshape(3, 125, elements)]
  transfers between devices with their start and end apart: 4 -> 0, of which waited for: 3 -> 0; matrix products, arithmetic and copies ran while one was open for 3% -> 0% of each run, Pallas kernels for 0% -> 0%
where the time goes in v1:
time: 37.2 us; the launch traced here: 36.7 us
  Pallas kernels  27.4 us (74%)
  local copies, waits for them, and re-layouts  9.21 us (25%)
    pallas_call x1, Pallas kernels, local(): pl.pallas_call(functools.partial(kernel, n_dom, n_sub, n_comp), out_shape...  27.4 us
    unnamed x23, local copies, waits for them, and re-layouts  9.21 us

profile of v1, /device:TPU:0, one launch (start us, length us, event | category | flops | bytes accessed | tf_op | source)
XLA Modules:
  0.0 36.7 jit_solution(13662812758232142345)
XLA Ops:
  0.0 0.0 copy-start
  0.0 1.0 %copy-done = bf16[128,1152]{1,0:T(8,128)(2,1)S(1)} copy-done((bf16[128,1152]{1,0:T(8,128)(2,1)S(1)}, bf16[128,1152]{1,0:T(8,128)(2,1)}, u32[]{:S(2)}) %copy-start) | copy-done | bytes 294936
  1.0 0.0 copy-start.1
  1.0 1.0 %copy-done.1 = bf16[384,384]{1,0:T(8,128)(2,1)S(1)} copy-done((bf16[384,384]{1,0:T(8,128)(2,1)S(1)}, bf16[384,384]{1,0:T(8,128)(2,1)}, u32[]{:S(2)}) %copy-start.1) | copy-done | bytes 294936
  1.9 0.0 copy-start.2
  1.9 0.9 %copy-done.2 = f32[3,8192]{1,0:T(4,128)S(1)} copy-done((f32[3,8192]{1,0:T(4,128)S(1)}, f32[3,8192]{1,0:T(4,128)}, u32[]{:S(2)}) %copy-start.2) | copy-done | bytes 98328
  2.8 0.0 copy-start.3
  2.8 0.8 %copy-done.3 = s32[125,128]{1,0:T(8,128)S(1)} copy-done((s32[125,128]{1,0:T(8,128)S(1)}, s32[125,128]{1,0:T(8,128)}, u32[]{:S(2)}) %copy-start.3) | copy-done | bytes 64024
  3.7 0.0 copy-start.4
  3.7 0.8 %copy-done.4 = bf16[125,128]{1,0:T(8,128)(2,1)S(1)} copy-done((bf16[125,128]{1,0:T(8,128)(2,1)S(1)}, bf16[125,128]{1,0:T(8,128)(2,1)}, u32[]{:S(2)}) %copy-start.4) | copy-done | bytes 32024
  4.4 0.0 copy-start.5
  4.4 0.8 %copy-done.5 = bf16[125,128]{1,0:T(8,128)(2,1)S(1)} copy-done((bf16[125,128]{1,0:T(8,128)(2,1)S(1)}, bf16[125,128]{1,0:T(8,128)(2,1)}, u32[]{:S(2)}) %copy-start.5) | copy-done | bytes 32024
  5.2 0.0 copy-start.6
  5.2 0.7 %copy-done.6 = f32[9,128]{1,0:T(8,128)S(1)} copy-done((f32[9,128]{1,0:T(8,128)S(1)}, f32[9,128]{1,0:T(8,128)}, u32[]{:S(2)}) %copy-start.6) | copy-done | bytes 4632
  5.9 0.0 copy-start.7
  5.9 0.7 %copy-done.7 = s32[4,64]{1,0:T(4,128)S(1)} copy-done((s32[4,64]{1,0:T(4,128)S(1)}, s32[4,64]{1,0:T(4,128)}, u32[]{:S(2)}) %copy-start.7) | copy-done | bytes 1048
  6.6 0.0 copy-start.8
  6.6 0.7 %copy-done.8 = s32[4,128]{1,0:T(4,128)S(1)} copy-done((s32[4,128]{1,0:T(4,128)S(1)}, s32[4,128]{1,0:T(4,128)}, u32[]{:S(2)}) %copy-start.8) | copy-done | bytes 2072
  7.2 0.0 copy-start.9
  7.2 0.7 %copy-done.9 = s32[4]{0:T(128)S(1)} copy-done((s32[4]{0:T(128)S(1)}, s32[4]{0:T(128)}, u32[]{:S(2)}) %copy-start.9) | copy-done | bytes 40
  7.9 0.0 copy-start.10
  7.9 0.7 %copy-done.10 = s32[4]{0:T(128)S(1)} copy-done((s32[4]{0:T(128)S(1)}, s32[4]{0:T(128)}, u32[]{:S(2)}) %copy-start.10) | copy-done | bytes 40
  8.6 27.4 %shard_map.109 = f32[3,8192]{1,0:T(4,128)S(1)} custom-call(s32[4]{0:T(128)S(1)} %copy-done.9, s32[4]{0:T(128)S(1)} %copy-done.10, f32[3,8192]{1,0:T(4,128)S(1)} %copy-done.2, s32[4,64]{1,0:T(4,128)S(1)} %copy-done.7, s32[4,128]{1,0:T(4,128)S(1)} %copy-done.8, s32[125,128]{1,0:T(8,128)S(1)} %copy-done.3, f32[9,128]{1,0:T(8,128)S(1)} %copy-done.6, ...), custom_call_target="tpu_custom_call" | custom-call | tf_op jit(solution)/shard_map/pallas_call | solution.py:445
  36.0 0.7 %copy.13 = f32[3,8192]{1,0:T(4,128)} copy(f32[3,8192]{1,0:T(4,128)S(1)} %shard_map.109) | data formatting | bytes 196608
Async XLA Ops:
  0.0 1.0 %copy-start = (bf16[128,1152]{1,0:T(8,128)(2,1)S(1)}, bf16[128,1152]{1,0:T(8,128)(2,1)}, u32[]{:S(2)}) copy-start(bf16[128,1152]{1,0:T(8,128)(2,1)} %constant.5.clone.bwd) | copy-start | bytes 884740
  1.0 1.0 %copy-start.1 = (bf16[384,384]{1,0:T(8,128)(2,1)S(1)}, bf16[384,384]{1,0:T(8,128)(2,1)}, u32[]{:S(2)}) copy-start(bf16[384,384]{1,0:T(8,128)(2,1)} %constant.4.clone.fwd) | copy-start | bytes 884740
  1.9 0.9 %copy-start.2 = (f32[3,8192]{1,0:T(4,128)S(1)}, f32[3,8192]{1,0:T(4,128)}, u32[]{:S(2)}) copy-start(f32[3,8192]{1,0:T(4,128)} %disp.1) | copy-start | bytes 294916
  2.8 0.8 %copy-start.3 = (s32[125,128]{1,0:T(8,128)S(1)}, s32[125,128]{1,0:T(8,128)}, u32[]{:S(2)}) copy-start(s32[125,128]{1,0:T(8,128)} %conn.1) | copy-start | bytes 192004
  3.7 0.8 %copy-start.4 = (bf16[125,128]{1,0:T(8,128)(2,1)S(1)}, bf16[125,128]{1,0:T(8,128)(2,1)}, u32[]{:S(2)}) copy-start(bf16[125,128]{1,0:T(8,128)(2,1)} %lame_first.1) | copy-start | bytes 96004
  4.4 0.8 %copy-start.5 = (bf16[125,128]{1,0:T(8,128)(2,1)S(1)}, bf16[125,128]{1,0:T(8,128)(2,1)}, u32[]{:S(2)}) copy-start(bf16[125,128]{1,0:T(8,128)(2,1)} %lame_shear.1) | copy-start | bytes 96004
  5.2 0.7 %copy-start.6 = (f32[9,128]{1,0:T(8,128)S(1)}, f32[9,128]{1,0:T(8,128)}, u32[]{:S(2)}) copy-start(f32[9,128]{1,0:T(8,128)} %jac.1) | copy-start | bytes 13828
  5.9 0.7 %copy-start.7 = (s32[4,64]{1,0:T(4,128)S(1)}, s32[4,64]{1,0:T(4,128)}, u32[]{:S(2)}) copy-start(s32[4,64]{1,0:T(4,128)} %far_lists.1) | copy-start | bytes 3076
  6.6 0.7 %copy-start.8 = (s32[4,128]{1,0:T(4,128)S(1)}, s32[4,128]{1,0:T(4,128)}, u32[]{:S(2)}) copy-start(s32[4,128]{1,0:T(4,128)} %near_lists.1) | copy-start | bytes 6148
  7.2 0.7 %copy-start.9 = (s32[4]{0:T(128)S(1)}, s32[4]{0:T(128)}, u32[]{:S(2)}) copy-start(s32[4]{0:T(128)} %far_counts.1) | copy-start | bytes 52
  7.9 0.7 %copy-start.10 = (s32[4]{0:T(128)S(1)}, s32[4]{0:T(128)}, u32[]{:S(2)}) copy-start(s32[4]{0:T(128)} %near_counts.1) | copy-start | bytes 52

commit v2 on v1

--- a/solution.py
+++ b/solution.py
@@ -116,6 +116,25 @@
     n_dom,
     n_sub,
     n_comp,
+    *refs,
+):
+    sources = refs[:11]
+    loads = refs[-1]
+    landed = refs[12:23]
+    copies = [
+        pltpu.make_async_copy(source, target, loads.at[at])
+        for at, (source, target) in enumerate(zip(sources, landed))
+    ]
+    for copy in copies:
+        copy.start()
+    body(n_dom, n_sub, n_comp, copies, *landed, refs[11], *refs[23:-1])
+
+
+def body(
+    n_dom,
+    n_sub,
+    n_comp,
+    copies,
     far_counts,
     near_counts,
     disp,
@@ -201,6 +220,9 @@
     lane8 = lax.broadcasted_iota(jnp.int32, (8, LANES), 1)
     lane = lax.broadcasted_iota(jnp.int32, (1, LANES), 1)
 
+    for copy in copies[:5]:
+        copy.wait()
+
     for c in range(3):
         tab[c, owned:, :] = jnp.zeros((LANES - owned, LANES), F32)
         for h in range(owned):
@@ -243,6 +265,9 @@
     sends = far_copies(far_out, far_in, send_far, recv_far)
     for copy in sends:
         copy.start()
+
+    for copy in copies[5:]:
+        copy.wait()
 
     tab_rows = jnp.full((8, LANES), NOWHERE, jnp.int32)
     index[0, 120:128, :] = tab_rows
@@ -438,16 +463,32 @@
 ):
     n_peers = n_sub * n_comp
     fwd, bwd = split_tables()
-    smem = pl.BlockSpec(memory_space=pltpu.SMEM)
-    vmem = pl.BlockSpec(memory_space=pltpu.VMEM)
+    operands = (
+        far_counts,
+        near_counts,
+        displacement,
+        far_lists,
+        near_lists,
+        connectivity,
+        inverse_jacobian,
+        lame_first,
+        lame_shear,
+        jnp.asarray(fwd),
+        jnp.asarray(bwd),
+    )
     far_slots = pltpu.VMEM((n_dom, 8, LANES), F32)
     near_slots = pltpu.VMEM((n_peers, 8, LANES), F32)
     return pl.pallas_call(
         functools.partial(kernel, n_dom, n_sub, n_comp),
         out_shape=jax.ShapeDtypeStruct(displacement.shape, F32),
-        in_specs=[smem] * 2 + [vmem] * 9,
-        out_specs=vmem,
+        in_specs=[pl.BlockSpec(memory_space=pltpu.HBM)] * 11,
+        out_specs=pl.BlockSpec(memory_space=pltpu.VMEM),
         scratch_shapes=[
+            pltpu.SMEM(operands[0].shape, jnp.int32),
+            pltpu.SMEM(operands[1].shape, jnp.int32),
+        ]
+        + [pltpu.VMEM(x.shape, x.dtype) for x in operands[2:]]
+        + [
             pltpu.VMEM((3, LANES, LANES), F32),
             pltpu.VMEM((3 * LANES, 2 * LANES), BF16),
             pltpu.VMEM((max(8, n_dom), LANES), jnp.int32),
@@ -468,23 +509,12 @@
         ]
         + [pltpu.SemaphoreType.DMA((n_dom,))] * 2
         + [pltpu.SemaphoreType.DMA((n_peers,))] * 4
-        + [pltpu.SemaphoreType.DMA((n_dom,))] * 2,
+        + [pltpu.SemaphoreType.DMA((n_dom,))] * 2
+        + [pltpu.SemaphoreType.DMA((11,))],
         compiler_params=pltpu.CompilerParams(
             collective_id=0, has_side_effects=True, vmem_limit_bytes=32 * 1024 * 1024
         ),
-    )(
-        far_counts,
-        near_counts,
-        displacement,
-        far_lists,
-        near_lists,
-        connectivity,
-        inverse_jacobian,
-        lame_first,
-        lame_shear,
-        jnp.asarray(fwd),
-        jnp.asarray(bwd),
-    )
+    )(*operands)
 
 
 def solution(mesh):

time: 37.2 us -> 37.1 us (level)
  no operation moved by 1% of the time
where the time goes in v2:
time: 37.1 us; the launch traced here: 36.7 us
  Pallas kernels  27.4 us (74%)
  local copies, waits for them, and re-layouts  9.21 us (25%)
    pallas_call x1, Pallas kernels, local(): pl.pallas_call(functools.partial(kernel, n_dom, n_sub, n_comp), out_shape...  27.4 us
    unnamed x23, local copies, waits for them, and re-layouts  9.21 us

profile of v2, /device:TPU:0, one launch (start us, length us, event | category | flops | bytes accessed | tf_op | source)
XLA Modules:
  0.0 36.7 jit_solution(11362212192237543779)
XLA Ops:
  0.0 0.0 copy-start
  0.0 1.0 %copy-done = bf16[128,1152]{1,0:T(8,128)(2,1)S(1)} copy-done((bf16[128,1152]{1,0:T(8,128)(2,1)S(1)}, bf16[128,1152]{1,0:T(8,128)(2,1)}, u32[]{:S(2)}) %copy-start) | copy-done | bytes 294936
  1.0 0.0 copy-start.1
  1.0 1.0 %copy-done.1 = bf16[384,384]{1,0:T(8,128)(2,1)S(1)} copy-done((bf16[384,384]{1,0:T(8,128)(2,1)S(1)}, bf16[384,384]{1,0:T(8,128)(2,1)}, u32[]{:S(2)}) %copy-start.1) | copy-done | bytes 294936
  1.9 0.0 copy-start.2
  1.9 0.9 %copy-done.2 = f32[3,8192]{1,0:T(4,128)S(1)} copy-done((f32[3,8192]{1,0:T(4,128)S(1)}, f32[3,8192]{1,0:T(4,128)}, u32[]{:S(2)}) %copy-start.2) | copy-done | bytes 98328
  2.8 0.0 copy-start.3
  2.8 0.8 %copy-done.3 = s32[125,128]{1,0:T(8,128)S(1)} copy-done((s32[125,128]{1,0:T(8,128)S(1)}, s32[125,128]{1,0:T(8,128)}, u32[]{:S(2)}) %copy-start.3) | copy-done | bytes 64024
  3.7 0.0 copy-start.4
  3.7 0.8 %copy-done.4 = bf16[125,128]{1,0:T(8,128)(2,1)S(1)} copy-done((bf16[125,128]{1,0:T(8,128)(2,1)S(1)}, bf16[125,128]{1,0:T(8,128)(2,1)}, u32[]{:S(2)}) %copy-start.4) | copy-done | bytes 32024
  4.4 0.0 copy-start.5
  4.4 0.8 %copy-done.5 = bf16[125,128]{1,0:T(8,128)(2,1)S(1)} copy-done((bf16[125,128]{1,0:T(8,128)(2,1)S(1)}, bf16[125,128]{1,0:T(8,128)(2,1)}, u32[]{:S(2)}) %copy-start.5) | copy-done | bytes 32024
  5.2 0.0 copy-start.6
  5.2 0.7 %copy-done.6 = f32[9,128]{1,0:T(8,128)S(1)} copy-done((f32[9,128]{1,0:T(8,128)S(1)}, f32[9,128]{1,0:T(8,128)}, u32[]{:S(2)}) %copy-start.6) | copy-done | bytes 4632
  5.9 0.0 copy-start.7
  5.9 0.7 %copy-done.7 = s32[4,64]{1,0:T(4,128)S(1)} copy-done((s32[4,64]{1,0:T(4,128)S(1)}, s32[4,64]{1,0:T(4,128)}, u32[]{:S(2)}) %copy-start.7) | copy-done | bytes 1048
  6.6 0.0 copy-start.8
  6.6 0.7 %copy-done.8 = s32[4,128]{1,0:T(4,128)S(1)} copy-done((s32[4,128]{1,0:T(4,128)S(1)}, s32[4,128]{1,0:T(4,128)}, u32[]{:S(2)}) %copy-start.8) | copy-done | bytes 2072
  7.2 0.0 copy-start.9
  7.2 0.7 %copy-done.9 = s32[4]{0:T(128)S(1)} copy-done((s32[4]{0:T(128)S(1)}, s32[4]{0:T(128)}, u32[]{:S(2)}) %copy-start.9) | copy-done | bytes 40
  7.9 0.0 copy-start.10
  7.9 0.7 %copy-done.10 = s32[4]{0:T(128)S(1)} copy-done((s32[4]{0:T(128)S(1)}, s32[4]{0:T(128)}, u32[]{:S(2)}) %copy-start.10) | copy-done | bytes 40
  8.6 27.4 %shard_map.109 = f32[3,8192]{1,0:T(4,128)S(1)} custom-call(s32[4]{0:T(128)S(1)} %copy-done.9, s32[4]{0:T(128)S(1)} %copy-done.10, f32[3,8192]{1,0:T(4,128)S(1)} %copy-done.2, s32[4,64]{1,0:T(4,128)S(1)} %copy-done.7, s32[4,128]{1,0:T(4,128)S(1)} %copy-done.8, s32[125,128]{1,0:T(8,128)S(1)} %copy-done.3, f32[9,128]{1,0:T(8,128)S(1)} %copy-done.6, ...), custom_call_target="tpu_custom_call" | custom-call | tf_op jit(solution)/shard_map/pallas_call | solution.py:481
  36.0 0.7 %copy.13 = f32[3,8192]{1,0:T(4,128)} copy(f32[3,8192]{1,0:T(4,128)S(1)} %shard_map.109) | data formatting | bytes 196608
Async XLA Ops:
  0.0 1.0 %copy-start = (bf16[128,1152]{1,0:T(8,128)(2,1)S(1)}, bf16[128,1152]{1,0:T(8,128)(2,1)}, u32[]{:S(2)}) copy-start(bf16[128,1152]{1,0:T(8,128)(2,1)} %constant.5.clone.refs_10_) | copy-start | bytes 884740
  1.0 1.0 %copy-start.1 = (bf16[384,384]{1,0:T(8,128)(2,1)S(1)}, bf16[384,384]{1,0:T(8,128)(2,1)}, u32[]{:S(2)}) copy-start(bf16[384,384]{1,0:T(8,128)(2,1)} %constant.4.clone.refs_9_) | copy-start | bytes 884740
  1.9 0.9 %copy-start.2 = (f32[3,8192]{1,0:T(4,128)S(1)}, f32[3,8192]{1,0:T(4,128)}, u32[]{:S(2)}) copy-start(f32[3,8192]{1,0:T(4,128)} %refs_2_.1) | copy-start | bytes 294916
  2.8 0.8 %copy-start.3 = (s32[125,128]{1,0:T(8,128)S(1)}, s32[125,128]{1,0:T(8,128)}, u32[]{:S(2)}) copy-start(s32[125,128]{1,0:T(8,128)} %refs_5_.1) | copy-start | bytes 192004
  3.7 0.8 %copy-start.4 = (bf16[125,128]{1,0:T(8,128)(2,1)S(1)}, bf16[125,128]{1,0:T(8,128)(2,1)}, u32[]{:S(2)}) copy-start(bf16[125,128]{1,0:T(8,128)(2,1)} %refs_7_.1) | copy-start | bytes 96004
  4.4 0.8 %copy-start.5 = (bf16[125,128]{1,0:T(8,128)(2,1)S(1)}, bf16[125,128]{1,0:T(8,128)(2,1)}, u32[]{:S(2)}) copy-start(bf16[125,128]{1,0:T(8,128)(2,1)} %refs_8_.1) | copy-start | bytes 96004
  5.2 0.7 %copy-start.6 = (f32[9,128]{1,0:T(8,128)S(1)}, f32[9,128]{1,0:T(8,128)}, u32[]{:S(2)}) copy-start(f32[9,128]{1,0:T(8,128)} %refs_6_.1) | copy-start | bytes 13828
  5.9 0.7 %copy-start.7 = (s32[4,64]{1,0:T(4,128)S(1)}, s32[4,64]{1,0:T(4,128)}, u32[]{:S(2)}) copy-start(s32[4,64]{1,0:T(4,128)} %refs_3_.1) | copy-start | bytes 3076
  6.6 0.7 %copy-start.8 = (s32[4,128]{1,0:T(4,128)S(1)}, s32[4,128]{1,0:T(4,128)}, u32[]{:S(2)}) copy-start(s32[4,128]{1,0:T(4,128)} %refs_4_.1) | copy-start | bytes 6148
  7.2 0.7 %copy-start.9 = (s32[4]{0:T(128)S(1)}, s32[4]{0:T(128)}, u32[]{:S(2)}) copy-start(s32[4]{0:T(128)} %refs_0_.1) | copy-start | bytes 52
  7.9 0.7 %copy-start.10 = (s32[4]{0:T(128)S(1)}, s32[4]{0:T(128)}, u32[]{:S(2)}) copy-start(s32[4]{0:T(128)} %refs_1_.1) | copy-start | bytes 52

commit v3 on v2

--- a/solution.py
+++ b/solution.py
@@ -12,8 +12,9 @@
 F32 = jnp.float32
 BF16 = jnp.bfloat16
 LANES = 128
+CAP_FAR = 64
 ROWS = 64
-NOWHERE = 16383
+NOWHERE = 1 << 20
 HIGH = 48
 MESH = pl.DeviceIdType.MESH
 
@@ -92,10 +93,10 @@
     return found
 
 
-def spread(rows, values):
+def spread(rows, values, height=HIGH):
     key = jnp.concatenate(rows, axis=1)
     low = onehot(2 * LANES, key & 255)
-    high = onehot(HIGH, key >> 8)
+    high = onehot(height, key >> 8)
     parts = []
     for c in range(3):
         top, rest = split(jnp.concatenate(values[c], axis=1))
@@ -108,8 +109,9 @@
     )
 
 
-def joined(acc, c):
-    return acc[2 * HIGH * c : 2 * HIGH * c + HIGH] + acc[2 * HIGH * c + HIGH : 2 * HIGH * (c + 1)]
+def joined(acc, c, height=HIGH):
+    start = 2 * height * c
+    return acc[start : start + height] + acc[start + height : start + 2 * height]
 
 
 def kernel(
@@ -149,6 +151,8 @@
     out,
     tab,
     table,
+    far_tab,
+    far_table,
     far_index,
     index,
     nodal,
@@ -174,29 +178,17 @@
     recv_back,
 ):
     n_peers = n_sub * n_comp
-    owned = disp.shape[1] // LANES
+    node_count = disp.shape[1]
+    owned = node_count // LANES
     dom = lax.axis_index("dom")
     peer = lax.axis_index("sub") * n_comp + lax.axis_index("comp")
 
-    def dom_id(step):
-        return {"dom": lax.rem(dom + step, n_dom)}
-
-    def peer_id(step):
+    far_rows_each = n_dom * CAP_FAR // LANES
+    others = [(d, t) for d in range(1, n_dom) for t in range(n_peers)]
+
+    def near_id(step):
         other = lax.rem(peer + step, n_peers)
         return {"sub": other // n_comp, "comp": lax.rem(other, n_comp)}
-
-    def far_copies(source, target, send, recv):
-        return [
-            pltpu.make_async_remote_copy(
-                src_ref=source.at[lax.rem(dom + step, n_dom)],
-                dst_ref=target.at[dom],
-                send_sem=send.at[step],
-                recv_sem=recv.at[step],
-                device_id=dom_id(step),
-                device_id_type=MESH,
-            )
-            for step in range(1, n_dom)
-        ]
 
     def near_copies(source, target, send, recv):
         return [
@@ -205,19 +197,36 @@
                 dst_ref=target.at[peer],
                 send_sem=send.at[step],
                 recv_sem=recv.at[step],
-                device_id=peer_id(step),
+                device_id=near_id(step),
                 device_id_type=MESH,
             )
             for step in range(1, n_peers)
         ]
 
+    def far_copies(source_at, target_at, send, recv):
+        return [
+            pltpu.make_async_remote_copy(
+                src_ref=source_at(d, lax.rem(peer + t, n_peers)),
+                dst_ref=target_at,
+                send_sem=send.at[d * n_peers + t],
+                recv_sem=recv.at[d * n_peers + t],
+                device_id=dict(near_id(t), dom=lax.rem(dom + d, n_dom)),
+                device_id_type=MESH,
+            )
+            for d, t in others
+        ]
+
     barrier = pltpu.get_barrier_semaphore()
-    for step in range(1, n_dom):
-        pl.semaphore_signal(barrier, inc=1, device_id=dom_id(step), device_id_type=MESH)
-    for step in range(1, n_peers):
-        pl.semaphore_signal(barrier, inc=1, device_id=peer_id(step), device_id_type=MESH)
-
-    lane8 = lax.broadcasted_iota(jnp.int32, (8, LANES), 1)
+    for d in range(n_dom):
+        for t in range(n_peers):
+            if d or t:
+                pl.semaphore_signal(
+                    barrier,
+                    inc=1,
+                    device_id=dict(near_id(t), dom=lax.rem(dom + d, n_dom)),
+                    device_id_type=MESH,
+                )
+
     lane = lax.broadcasted_iota(jnp.int32, (1, LANES), 1)
 
     for copy in copies[:5]:
@@ -228,13 +237,13 @@
         for h in range(owned):
             tab[c, h : h + 1, :] = disp[c : c + 1, h * LANES : (h + 1) * LANES]
 
-    def turn():
-        for c in range(3):
-            top, rest = split(tab[c].T)
+    def turn(source, table):
+        for c in range(3):
+            top, rest = split(source[c].T)
             table[c * LANES : (c + 1) * LANES, :LANES] = top
             table[c * LANES : (c + 1) * LANES, LANES:] = rest
 
-    turn()
+    turn(tab, table)
 
     far_index[...] = jnp.zeros_like(far_index)
     far_index[:n_dom, :64] = far_lists[...]
@@ -249,22 +258,44 @@
         for t in range(n_peers)
     ]
 
+    own_rows = [jnp.where(row < node_count, row, NOWHERE) for row in near_rows]
+    far_keys = [
+        jnp.where(
+            (row >= node_count) & (row < NOWHERE),
+            row + (peer * (n_dom * CAP_FAR) - node_count),
+            NOWHERE,
+        )
+        for row in near_rows
+    ]
+
     far_out[...] = jnp.zeros_like(far_out)
     near_out[...] = jnp.zeros_like(near_out)
     ghost_out[...] = jnp.zeros_like(ghost_out)
     back_out[...] = jnp.zeros_like(back_out)
 
-    found = pick(table[...], far_rows)
+    found = pick(table[...], far_rows + own_rows)
     for p in range(n_dom):
         for c in range(3):
             far_out[p, c : c + 1, :] = found[c][p]
-    far_in[dom] = jnp.zeros((8, LANES), F32)
-    back_in[dom] = jnp.zeros((8, LANES), F32)
-
-    pl.semaphore_wait(barrier, n_dom - 1 + n_peers - 1)
-    sends = far_copies(far_out, far_in, send_far, recv_far)
-    for copy in sends:
+    for t in range(n_peers):
+        for c in range(3):
+            near_out[t, c : c + 1, :] = found[c][n_dom + t]
+        near_out[t, 3:4, :] = far_keys[t].astype(F32)
+    for s in range(n_peers):
+        far_in[s, dom] = jnp.zeros((8, LANES), F32)
+        back_in[dom, s] = jnp.zeros((8, LANES), F32)
+
+    pl.semaphore_wait(barrier, n_dom * n_peers - 1)
+    far_sends = far_copies(
+        lambda d, t: far_out.at[lax.rem(dom + d, n_dom)],
+        far_in.at[peer, dom],
+        send_far,
+        recv_far,
+    )
+    near_sends = near_copies(near_out, near_in, send_near, recv_near)
+    for copy in far_sends + near_sends:
         copy.start()
+    near_in[peer] = near_out[peer]
 
     for copy in copies[5:]:
         copy.wait()
@@ -377,32 +408,25 @@
 
     gather(0)
 
-    for copy in sends:
+    elements(0)
+
+    far_tab[...] = jnp.zeros_like(far_tab)
+    for copy in far_sends + near_sends:
         copy.wait()
-    for j in range(n_dom // 2):
-        for c in range(3):
-            tab[c, owned + j : owned + j + 1, :] = jnp.where(
-                lane < 64, far_in[2 * j, c : c + 1, :], far_in[2 * j + 1, c : c + 1, :]
-            )
-    turn()
-    found = pick(table[...], near_rows)
-    for t in range(n_peers):
-        for c in range(3):
-            near_out[t, c : c + 1, :] = found[c][t]
-    near_in[peer] = near_out[peer]
-    sends = near_copies(near_out, near_in, send_near, recv_near)
-    for copy in sends:
-        copy.start()
-
-    elements(0)
-
-    for copy in sends:
-        copy.wait()
+    for s in range(n_peers):
+        for j in range(far_rows_each):
+            at = s * far_rows_each + j
+            for c in range(3):
+                far_tab[c, at : at + 1, :] = jnp.where(
+                    lane < 64, far_in[s, 2 * j, c : c + 1, :], far_in[s, 2 * j + 1, c : c + 1, :]
+                )
+    turn(far_tab, far_table)
+    ghost_keys = [near_in[s, 3:4, :].astype(jnp.int32) for s in range(n_peers)]
+    found = pick(far_table[...], ghost_keys)
     for c in range(3):
-        tab[c, owned:, :] = jnp.zeros((LANES - owned, LANES), F32)
         for s in range(n_peers):
-            tab[c, owned + s : owned + s + 1, :] = near_in[s, c : c + 1, :]
-    turn()
+            tab[c, owned + s : owned + s + 1, :] = near_in[s, c : c + 1, :] + found[c][s]
+    turn(tab, table)
     gather(1)
     elements(1)
     scatter(1, acc_out)
@@ -413,33 +437,46 @@
         for s in range(n_peers):
             half = (s % 2) * LANES
             ghost_out[s, c : c + 1, :] = whole[kept + s // 2 : kept + s // 2 + 1, half : half + LANES]
-    ghost_in[peer] = ghost_out[peer]
-    sends = near_copies(ghost_out, ghost_in, send_ghost, recv_ghost)
+    far_height = -(-n_peers * n_dom * CAP_FAR // (2 * LANES) // 16) * 16
+    beyond = spread(
+        ghost_keys,
+        [[ghost_out[s, c : c + 1, :] for s in range(n_peers)] for c in range(3)],
+        far_height,
+    )
+    for c in range(3):
+        whole = joined(beyond, c, far_height)
+        for s in range(n_peers):
+            for p in range(n_dom):
+                row = s * (far_rows_each // 2) + p // 4
+                half = ((p // 2) % 2) * LANES
+                back_out[p, s, c : c + 1, :] = whole[row : row + 1, half : half + LANES]
+    sends = near_copies(ghost_out, ghost_in, send_ghost, recv_ghost) + far_copies(
+        lambda d, t: back_out.at[lax.rem(dom + d, n_dom), t],
+        back_in.at[dom, peer],
+        send_back,
+        recv_back,
+    )
     for copy in sends:
         copy.start()
+    ghost_in[peer] = ghost_out[peer]
 
     scatter(0, acc_in)
+    mine = (lane >> 6) == lax.rem(dom, 2)
+    back_rows = [jnp.where(mine, far_rows[p], NOWHERE) for p in range(n_dom)]
 
     for copy in sends:
         copy.wait()
-    ghost = spread(
-        near_rows, [[ghost_in[t, c : c + 1, :] for t in range(n_peers)] for c in range(3)]
-    )
-    for c in range(3):
-        whole = joined(ghost, c)
-        for p in range(n_dom):
-            half = ((p // 2) % 2) * LANES
-            back_out[p, c : c + 1, :] = whole[kept + p // 4 : kept + p // 4 + 1, half : half + LANES]
-    sends = far_copies(back_out, back_in, send_back, recv_back)
-    for copy in sends:
-        copy.start()
-    total = acc_in[...] + acc_out[...] + ghost
-    mine = (lane >> 6) == lax.rem(dom, 2)
-    back_rows = [jnp.where(mine, far_rows[p], NOWHERE) for p in range(n_dom)]
-    for copy in sends:
-        copy.wait()
+    arrived = [back_in[p, 0] for p in range(n_dom)]
+    for t in range(1, n_peers):
+        arrived = [arrived[p] + back_in[p, t] for p in range(n_dom)]
+    total = acc_in[...] + acc_out[...]
     total = total + spread(
-        back_rows, [[back_in[p, c : c + 1, :] for p in range(n_dom)] for c in range(3)]
+        own_rows + back_rows,
+        [
+            [ghost_in[t, c : c + 1, :] for t in range(n_peers)]
+            + [arrived[p][c : c + 1, :] for p in range(n_dom)]
+            for c in range(3)
+        ],
     )
     for c in range(3):
         whole = joined(total, c)
@@ -476,7 +513,6 @@
         jnp.asarray(fwd),
         jnp.asarray(bwd),
     )
-    far_slots = pltpu.VMEM((n_dom, 8, LANES), F32)
     near_slots = pltpu.VMEM((n_peers, 8, LANES), F32)
     return pl.pallas_call(
         functools.partial(kernel, n_dom, n_sub, n_comp),
@@ -491,6 +527,8 @@
         + [
             pltpu.VMEM((3, LANES, LANES), F32),
             pltpu.VMEM((3 * LANES, 2 * LANES), BF16),
+            pltpu.VMEM((3, LANES, LANES), F32),
+            pltpu.VMEM((3 * LANES, 2 * LANES), BF16),
             pltpu.VMEM((max(8, n_dom), LANES), jnp.int32),
             pltpu.VMEM((2, 2 * ROWS, LANES), jnp.int32),
             pltpu.VMEM((3, 2 * ROWS, LANES), F32),
@@ -498,21 +536,21 @@
             pltpu.VMEM((LANES, LANES), F32),
             pltpu.VMEM((6 * HIGH, 2 * LANES), F32),
             pltpu.VMEM((6 * HIGH, 2 * LANES), F32),
-            far_slots,
-            far_slots,
+            pltpu.VMEM((n_dom, 8, LANES), F32),
+            pltpu.VMEM((n_peers, n_dom, 8, LANES), F32),
             near_slots,
             near_slots,
             near_slots,
             near_slots,
-            far_slots,
-            far_slots,
+            pltpu.VMEM((n_dom, n_peers, 8, LANES), F32),
+            pltpu.VMEM((n_dom, n_peers, 8, LANES), F32),
         ]
-        + [pltpu.SemaphoreType.DMA((n_dom,))] * 2
+        + [pltpu.SemaphoreType.DMA((n_dom * n_peers,))] * 2
         + [pltpu.SemaphoreType.DMA((n_peers,))] * 4
-        + [pltpu.SemaphoreType.DMA((n_dom,))] * 2
+        + [pltpu.SemaphoreType.DMA((n_dom * n_peers,))] * 2
         + [pltpu.SemaphoreType.DMA((11,))],
         compiler_params=pltpu.CompilerParams(
-            collective_id=0, has_side_effects=True, vmem_limit_bytes=32 * 1024 * 1024
+            collective_id=0, has_side_effects=True
         ),
     )(*operands)
 

time: 37.1 us -> 26.1 us (0.70)
  local copies, waits for them, and re-layouts: 9.21 us -> 1.58 us
  Pallas kernels: 27.4 us -> 24.3 us
    unnamed x23 -> x1, local copies, waits for them, and re-layouts: 9.21 us -> 1.58 us
    pallas_call x1, Pallas kernels: 27.4 us -> 24.3 us  [local(): pl.pallas_call(functools.partial(kernel, n_dom, n_sub, n_comp), out_shape...]
where the time goes in v3:
time: 26.1 us; the launch traced here: 25.9 us
  Pallas kernels  24.3 us (93%)
  local copies, waits for them, and re-layouts  1.58 us (6%)
    pallas_call x1, Pallas kernels, local(): pl.pallas_call(functools.partial(kernel, n_dom, n_sub, n_comp), out_shape...  24.3 us
    unnamed x1, local copies, waits for them, and re-layouts  1.58 us

profile of v3, /device:TPU:0, one launch (start us, length us, event | category | flops | bytes accessed | tf_op | source)
XLA Modules:
  0.0 25.9 jit_solution(4428732141002823173)
XLA Ops:
  0.0 24.3 %shard_map.109 = f32[3,8192]{1,0:T(4,128)} custom-call(s32[4]{0:T(128)} %refs_0_.1, s32[4]{0:T(128)} %refs_1_.1, f32[3,8192]{1,0:T(4,128)} %refs_2_.1, s32[4,64]{1,0:T(4,128)} %refs_3_.1, s32[4,128]{1,0:T(4,128)} %refs_4_.1, s32[125,128]{1,0:T(8,128)} %refs_5_.1, f32[9,128]{1,0:T(8,128)} %refs_6_.1, bf16[125,128]{1,0:T(8,128)(2,1)} %refs_7_.1, ...), custom_call_target="tpu_custom_call" | custom-call | tf_op jit(solution)/shard_map/pallas_call | solution.py:517
  24.3 1.6 %copy.13 = f32[3,8192]{1,0:T(4,128)} copy(f32[3,8192]{1,0:T(4,128)} %shard_map.109) | data formatting | bytes 196608

commit v4 on v3

--- a/solution.py
+++ b/solution.py
@@ -73,8 +73,9 @@
 
 
 def onehot(rows, key):
-    grid = lax.broadcasted_iota(jnp.int32, (rows, key.shape[1]), 0)
-    return jnp.where(grid == key, 1.0, 0.0).astype(BF16)
+    grid = lax.broadcasted_iota(jnp.int32, (rows, key.shape[1]), 0).astype(F32).astype(BF16)
+    name = key.astype(F32).astype(BF16)
+    return jnp.where(grid == name, jnp.ones((), BF16), jnp.zeros((), BF16))
 
 
 def pick(table, rows):

time: 26.1 us -> 25.9 us (level)
  no operation moved by 1% of the time
where the time goes in v4:
time: 25.9 us; the launch traced here: 25.8 us
  Pallas kernels  24.2 us (93%)
  local copies, waits for them, and re-layouts  1.58 us (6%)
    pallas_call x1, Pallas kernels, local(): pl.pallas_call(functools.partial(kernel, n_dom, n_sub, n_comp), out_shape...  24.2 us
    unnamed x1, local copies, waits for them, and re-layouts  1.58 us

profile of v4, /device:TPU:0, one launch (start us, length us, event | category | flops | bytes accessed | tf_op | source)
XLA Modules:
  0.0 25.8 jit_solution(12225092953329724312)
XLA Ops:
  0.0 24.2 %shard_map.109 = f32[3,8192]{1,0:T(4,128)} custom-call(s32[4]{0:T(128)} %refs_0_.1, s32[4]{0:T(128)} %refs_1_.1, f32[3,8192]{1,0:T(4,128)} %refs_2_.1, s32[4,64]{1,0:T(4,128)} %refs_3_.1, s32[4,128]{1,0:T(4,128)} %refs_4_.1, s32[125,128]{1,0:T(8,128)} %refs_5_.1, f32[9,128]{1,0:T(8,128)} %refs_6_.1, bf16[125,128]{1,0:T(8,128)(2,1)} %refs_7_.1, ...), custom_call_target="tpu_custom_call" | custom-call | tf_op jit(solution)/shard_map/pallas_call | solution.py:518
  24.2 1.6 %copy.13 = f32[3,8192]{1,0:T(4,128)} copy(f32[3,8192]{1,0:T(4,128)} %shard_map.109) | data formatting | bytes 196608
